TPU v7x, 128 devices: a whole 4x4x4 slice. The times are simulated.
128 devices in a mesh: ctx: 16 (over y, x), head: 8 (over z, core).
Axes of the slice: x: 4, y: 4, z: 4, core: 2. Of those that a mesh axis runs over, the one named last changes fastest.
Arguments:
- q_nope: bfloat16 [8, 128, 128], P(None, 'head'), may hold values from -6 to 6
- q_rope: bfloat16 [8, 128, 64], P(None, 'head'), may hold values from -10 to 10
- latent_cache: bfloat16 [8, 131072, 576], P(None, 'ctx'), may hold values from -8 to 8
- lengths: int32 [8], replicated, may hold values from 16384 to 131072, as said below
- w_key_absorb: bfloat16 [128, 128, 512], P('head'), may hold values from -0.5 to 0.5
- w_value_up: bfloat16 [128, 512, 128], P('head'), may hold values from -0.25 to 0.25
- w_output: bfloat16 [16384, 7168], P('head', 'ctx'), may hold values from -0.046875 to 0.046875
- w_gate: bfloat16 [16, 7168, 2048], P('ctx', None, 'head'), may hold values from -0.0625 to 0.0625
- w_up: bfloat16 [16, 7168, 2048], P('ctx', None, 'head'), may hold values from -0.0625 to 0.0625
- w_down: bfloat16 [16, 2048, 7168], P('ctx', 'head'), may hold values from -0.125 to 0.125
- expert_ids: int32 [8, 8], replicated, may hold values from 0 to 15, all different within a row
- gate_weights: float32 [8, 8], replicated, may hold values from 0.05 to 0.4
Outputs:
- attn_out: bfloat16 [8, 7168], P(None, 'ctx')
- expert_out: bfloat16 [8, 7168], P(None, ('ctx', 'head'))
Inputs may be any that keep to these rules, and one draw needn't show every extreme that they name: `lengths`: every row has at least 16384 valid positions and row 0 has all of them.
All inputs are finite; a program needn't handle non-finite values.
Results may differ from a plain program's by a relative error of at most 0.03.
Values may be sent and summed in bfloat16 or wider, within the bound.
A program may use at most 192 MiB of HBM per device.

v0:
```python
import jax
import jax.numpy as jnp
from jax import lax
from jax.sharding import PartitionSpec as P

NOPE = 128
ROPE = 64
LAT = 512


def merged(part, axis, combine):
    gathered = jax.tree.map(lambda a: lax.all_gather(a, axis), part)

    def take(source):
        return jax.tree.map(lambda a: lax.dynamic_index_in_dim(a, source, 0, False), gathered)

    return lax.fori_loop(
        1, lax.axis_size(axis), lambda source, state: combine(state, take(source)), take(0)
    )


def join_partials(first, second):
    peak = jnp.maximum(first[0], second[0])
    left = jnp.exp(first[0] - peak)
    right = jnp.exp(second[0] - peak)
    total = first[1] * left + second[1] * right
    summed = first[2] * left[..., None] + second[2] * right[..., None]
    return (peak, total, summed)


def attend(query, cache, row_lengths, offset):
    scale = (NOPE + ROPE) ** (-0.5)
    span = cache.shape[1]
    positions = offset + jnp.arange(span, dtype=jnp.int32)
    score = jnp.einsum("bhc,btc->bht", query, cache, preferred_element_type=jnp.float32) * scale
    valid = positions[None, None, :] < row_lengths[:, None, None]
    peak = jnp.max(jnp.where(valid, score, -1e30), axis=-1)
    weight = jnp.where(valid, jnp.exp(score - peak[..., None]), 0.0)
    total = jnp.sum(weight, axis=-1)
    summed = jnp.einsum(
        "bht,btl->bhl",
        weight.astype(jnp.bfloat16),
        cache[:, :, :LAT],
        preferred_element_type=jnp.float32,
    )
    return (peak, total, summed)


def combine_slices(peak, total, summed):
    peak, total, summed = merged((peak, total, summed), "ctx", join_partials)
    return (summed / total[..., None]).astype(jnp.bfloat16)


def body(
    q_nope,
    q_rope,
    latent_cache,
    lengths,
    w_key_absorb,
    w_value_up,
    w_output,
    w_gate,
    w_up,
    w_down,
    expert_ids,
    gate_weights,
):
    rows = q_nope.shape[0]
    q_latent = jnp.einsum(
        "bhn,hnl->bhl", q_nope, w_key_absorb, preferred_element_type=jnp.float32
    ).astype(jnp.bfloat16)
    query = jnp.concatenate([q_latent, q_rope], axis=-1)
    offset = lax.axis_index("ctx") * latent_cache.shape[1]
    peak, total, summed = attend(query, latent_cache, lengths, offset)
    o_latent = combine_slices(peak, total, summed)
    head_out = jnp.einsum(
        "bhl,hln->bhn", o_latent, w_value_up, preferred_element_type=jnp.float32
    ).astype(jnp.bfloat16)
    head_out = head_out.reshape(rows, -1)
    partial_proj = jnp.dot(head_out, w_output, preferred_element_type=jnp.float32)
    attn_out = lax.psum(partial_proj, "head").astype(jnp.bfloat16)
    features = lax.all_gather(attn_out, "ctx", axis=1, tiled=True)
    wide = features.astype(jnp.float32)
    normed = (wide / jnp.sqrt(jnp.mean(wide * wide, axis=-1, keepdims=True) + 1e-06)).astype(
        jnp.bfloat16
    )
    mine = lax.axis_index("ctx")
    select = jnp.sum(gate_weights * (expert_ids == mine).astype(jnp.float32), axis=1)
    gate = jnp.dot(normed, w_gate[0], preferred_element_type=jnp.float32)
    upper = jnp.dot(normed, w_up[0], preferred_element_type=jnp.float32)
    hidden = (jax.nn.silu(gate) * upper).astype(jnp.bfloat16)
    result = jnp.dot(hidden, w_down[0], preferred_element_type=jnp.float32) * select[:, None]
    expert_out = lax.psum_scatter(result, ("ctx", "head"), scatter_dimension=1, tiled=True).astype(
        jnp.bfloat16
    )
    return (attn_out, expert_out)


def solution(mesh):
    return jax.shard_map(
        body,
        mesh=mesh,
        in_specs=(
            P(None, "head", None),
            P(None, "head", None),
            P(None, "ctx", None),
            P(),
            P("head", None, None),
            P("head", None, None),
            P("head", "ctx"),
            P("ctx", None, "head"),
            P("ctx", None, "head"),
            P("ctx", "head", None),
            P(),
            P(),
        ),
        out_specs=(P(None, "ctx"), P(None, ("ctx", "head"))),
        check_vma=False,
    )
```

profile of v0, /device:TPU:1, one launch (start us, length us, event | category | flops | bytes accessed | tf_op | source)
XLA Modules:
  0.0 271.2 jit_solution(7608450080655570873)
XLA Ops:
  7.2 0.0 copy-start
  7.2 0.0 all-gather.6.cloned.1.call-start
  7.2 0.9 copy.20
  8.2 0.8 broadcast_compare_fusion
  8.9 0.0 copy-done
  8.9 1.1 fusion.16
  10.1 28.7 %select_reduce_fusion = (f32[8,16]{1,0:T(8,128)S(1)}, f32[8,16,8192]{2,1,0:T(8,128)}) fusion(pred[8,8192]{1,0:T(8,128)(4,1)S(1)} %broadcast_compare_fusion, bf16[8,8192,576]{1,2,0:T(8,128)(2,1)} %param.16, bf16[8,16,576]{2,0,1:T(8,128)(2,1)S(1)} %pad_maximum_fusion), kind=kOutput, calls=%fused_computation.13 | convolution fusion | flops 1211105152 | bytes 79905280 | tf_op jit(solution)/shard_map/bhc,btc->bht/dot_general | solution.py:35
  38.8 27.1 %fusion.3 = f32[8,16,512]{2,1,0:T(8,128)} fusion(bf16[8,8192,576]{1,2,0:T(8,128)(2,1)} %param.16, f32[8,16,8192]{2,1,0:T(8,128)} %get-tuple-element.200, f32[8,16]{1,0:T(8,128)S(1)} %get-tuple-element.199, pred[8,8192]{1,0:T(8,128)(4,1)S(1)} %broadcast_compare_fusion), kind=kOutput, calls=%fused_computation.8 | convolution fusion | flops 1076887552 | bytes 71631360 | tf_op jit(solution)/shard_map/bht,btl->bhl/dot_general | solution.py:40
  65.9 0.0 copy-start.2
  65.9 0.0 copy-start.3
  65.9 0.0 all-gather.6.cloned.1.call-update
  66.0 19.7 %all-gather = f32[128,16]{1,0:T(8,128)S(1)} all-gather(f32[8,16]{1,0:T(8,128)S(1)} %get-tuple-element.199), channel_id=2, replica_groups=mesh['ctx'=16,'head'=8] {'ctx'}, dimensions={0}, use_global_device_ids=true | all-gather | bytes 8704 | tf_op jit(solution)/shard_map/all_gather | solution.py:12
  85.7 3.3 %fusion.11 = f32[8,16]{1,0:T(8,128)S(1)} fusion(f32[8,16,8192]{2,1,0:T(8,128)} %get-tuple-element.200, f32[8,16]{1,0:T(8,128)S(1)} %get-tuple-element.199, pred[8,8192]{1,0:T(8,128)(4,1)S(1)} %broadcast_compare_fusion), kind=kLoop, calls=%fused_computation.20 | loop fusion | flops 3145600 | bytes 4260864 | tf_op jit(solution)/shard_map/reduce_sum | solution.py:39
  89.0 18.5 %all-gather.1 = f32[128,16]{1,0:T(8,128)S(1)} all-gather(f32[8,16]{1,0:T(8,128)S(1)} %fusion.11), channel_id=3, replica_groups=mesh['ctx'=16,'head'=8] {'ctx'}, dimensions={0}, use_global_device_ids=true | all-gather | bytes 8704 | tf_op jit(solution)/shard_map/all_gather | solution.py:12
  107.5 0.0 copy-done.2
  107.5 0.0 copy-done.3
  107.5 0.1 select_reduce_fusion.1
  107.6 13.5 %all-gather.6.cloned.1.call-done = f32[128,16,512]{2,1,0:T(8,128)} async-done(((f32[8,16,512]{2,1,0:T(8,128)}), f32[128,16,512]{2,1,0:T(8,128)}) %all-gather.6.cloned.1.call-update) | async-done | bytes 4194320 | tf_op jit(solution)/shard_map/all_gather | solution.py:12
  121.2 1.0 slice.12
  122.1 16.8 %while.19 = (s32[]{:T(128)}, f32[8,16]{1,0:T(8,128)S(1)}, f32[8,16]{1,0:T(8,128)S(1)}, f32[8,16,512]{2,1,0:T(8,128)S(1)}, f32[16,8,16]{2,1,0:T(8,128)S(1)}, /*in...) while((s32[]{:T(128)}, f32[8,16]{1,0:T(8,128)S(1)}, ...), condition=%wide.region_3.4_spmd, body=%wide.region_2.3_spmd.sunk | while | flops 197381 | bytes 791703 | solution.py:17
  122.2 1.1 fusion.47
  123.3 1.1 fusion.47
  124.4 1.1 fusion.47
  125.5 1.1 fusion.47
  126.7 1.1 fusion.47
  127.8 1.1 fusion.47
  128.9 1.1 fusion.47
  130.0 1.1 fusion.47
  131.1 1.1 fusion.47
  132.3 1.1 fusion.47
  133.4 1.1 fusion.47
  134.5 1.1 fusion.47
  135.6 1.1 fusion.47
  136.7 1.1 fusion.47
  137.9 1.1 fusion.47
  139.0 0.1 divide_convert_fusion
  139.1 3.0 %fusion.26 = f32[8,448]{1,0:T(8,128)S(1)} fusion(bf16[2048,448]{0,1:T(8,128)(2,1)} %param.20, bf16[16,512,128]{2,1,0:T(8,128)(2,1)} %param.19, bf16[8,16,512]{2,1,0:T(8,128)(2,1)S(1)} %divide_convert_fusion), kind=kOutput, calls=%fused_computation.30 | convolution fusion | flops 31473664 | bytes 4077568 | tf_op jit(solution)/shard_map/dot_general | solution.py:80
  142.1 22.9 %psum.7 = bf16[8,448]{1,0:T(8,128)(2,1)S(1)} all-reduce(f32[8,448]{1,0:T(8,128)S(1)} %fusion.26), channel_id=1, replica_groups=mesh['ctx'=16,'head'=8] {'head'}, use_global_device_ids=true, to_apply=%region_4.5 | all-reduce | flops 3584 | bytes 21504 | tf_op jit(solution)/shard_map/psum | solution.py:81
  165.0 0.0 copy-start.1
  165.0 18.3 %all-gather.3 = bf16[16,448,8]{1,2,0:T(8,128)(2,1)S(1)} all-gather(bf16[1,448,8]{1,2,0:T(8,128)(2,1)S(1)} %bitcast.59), channel_id=1, replica_groups=mesh['ctx'=16,'head'=8] {'ctx'}, dimensions={0}, use_global_device_ids=true | all-gather | bytes 121856 | tf_op jit(solution)/shard_map/all_gather | solution.py:82
  183.4 0.1 reshape.65
  183.5 0.2 multiply_reduce_fusion
  183.7 2.7 fusion.8
  186.3 5.3 %convolution_multiply_fusion.1 = f32[8,7168]{1,0:T(8,128)S(1)} fusion(bf16[1,256,7168]{2,1,0:T(8,128)(2,1)} %param.23, bf16[1,7168,256]{2,1,0:T(8,128)(2,1)} %param.22, f32[8]{0:T(128)S(1)} %select_reduce_fusion.1, f32[8,256]{1,0:T(8,128)S(1)} %fusion.8, f32[7168,8]{0,1:T(8,128)S(1)} %reshape.65, f32[8]{0:T(128)S(1)} %add_sqrt_fusion), kind=kOutput, calls=%fused_computation.11 | convolution fusion | flops 58904576 | bytes 7807040 | tf_op jit(solution)/shard_map/dot_general | solution.py:92
  191.6 0.0 copy-done.1
  191.6 72.1 %all-reduce.2 = bf16[8,7168]{1,0:T(8,128)(2,1)S(1)} all-reduce(f32[8,7168]{1,0:T(8,128)S(1)} %convolution_multiply_fusion.1), channel_id=5, replica_groups=mesh['ctx'=16,'head'=8] {'ctx','head'}, use_global_device_ids=true, to_apply=%region_7.8.clone | all-reduce | flops 57344 | bytes 344064
  263.7 0.7 dynamic-slice_convert_fusion
  (21 shorter events, 0.3 us)
Async XLA Ops:
  7.2 1.8 copy-start
  7.2 114.0 %all-gather.6.cloned.1.call-start = ((), (), s32[]{:S(2)}) async-start(), calls=%async_computation | async-start | bytes 4456448 | tf_op jit(solution)/shard_map/all_gather | solution.py:12
  65.9 41.6 %copy-start.2 = (f32[8,8]{1,0:T(8,128)S(1)}, f32[8,8]{1,0:T(8,128)}, u32[]{:S(2)}) copy-start(f32[8,8]{1,0:T(8,128)} %param.25) | copy-start | bytes 772
  65.9 41.6 %copy-start.3 = (s32[8,8]{1,0:T(8,128)S(1)}, s32[8,8]{1,0:T(8,128)}, u32[]{:S(2)}) copy-start(s32[8,8]{1,0:T(8,128)} %param.24) | copy-start | bytes 772
  165.0 26.6 %copy-start.1 = (bf16[8,448]{1,0:T(8,128)(2,1)}, bf16[8,448]{1,0:T(8,128)(2,1)S(1)}, u32[]{:S(2)}) copy-start(bf16[8,448]{1,0:T(8,128)(2,1)S(1)} %psum.7) | copy-start | bytes 21508
Sparse Core Ops, SparseCore 0:
  66.1 55.0 all-gather.5
where the time goes:
time: 272 us; the launch traced here: 271 us
  blocking collectives  152 us (56%)
  matrix products  67.9 us (25%)
  other arithmetic  20.8 us (8%)
  between operations  14.1 us (5%)
  waiting for transfers between devices  13.5 us (5%)
  local copies, waits for them, and re-layouts  2.74 us (1%)
    unnamed x1, blocking collectives  72.1 us
    all_gather x2, blocking collectives, merged(): gathered = jax.tree.map(lambda a: lax.all_gather(a, axis), part)  38.2 us
    dot_general x1, matrix products, attend(): jnp.einsum('bhc,btc->bht', query, cache, preferred_element_type=jnp.float32)  28.7 us
    dot_general x1, matrix products, attend(): jnp.einsum('bht,btl->bhl', weight.astype(jnp.bfloat16), cache[:, :, :LAT]...  27.1 us
    psum x1, blocking collectives, body(): attn_out = lax.psum(partial_proj, 'head').astype(jnp.bfloat16)  22.9 us
    all_gather x1, blocking collectives, body(): features = lax.all_gather(attn_out, 'ctx', axis=1, tiled=True)  18.3 us
    add x15, other arithmetic, join_partials(): summed = first[2] * left[..., None] + second[2] * right[..., None]  16.1 us
    all_gather x1, waiting for transfers between devices, merged(): gathered = jax.tree.map(lambda a: lax.all_gather(a, axis), part)  13.5 us
  transfers between devices with their start and end apart: 1, of which 1 were waited for; matrix products, arithmetic and copies ran while one was open for 1% of the time, Pallas kernels for 0%

commit v1 on v0

--- a/solution.py
+++ b/solution.py
@@ -6,6 +6,12 @@
 NOPE = 128
 ROPE = 64
 LAT = 512
+
+
+def summed_here(block, axis):
+    parts = lax.all_gather(block, axis, axis=0, tiled=False)
+    acc = parts.sum(axis=0)
+    return acc
 
 
 def merged(part, axis, combine):
@@ -78,7 +84,7 @@
     ).astype(jnp.bfloat16)
     head_out = head_out.reshape(rows, -1)
     partial_proj = jnp.dot(head_out, w_output, preferred_element_type=jnp.float32)
-    attn_out = lax.psum(partial_proj, "head").astype(jnp.bfloat16)
+    attn_out = summed_here(partial_proj, "head").astype(jnp.bfloat16)
     features = lax.all_gather(attn_out, "ctx", axis=1, tiled=True)
     wide = features.astype(jnp.float32)
     normed = (wide / jnp.sqrt(jnp.mean(wide * wide, axis=-1, keepdims=True) + 1e-06)).astype(

time: 272 us -> 260 us (0.956)
  blocking collectives: 152 us -> 139 us
    psum x1 -> x0, blocking collectives: 22.9 us -> none  [body(): attn_out = lax.psum(partial_proj, 'head').astype(jnp.bfloat16)]
    all_gather x0 -> x1, blocking collectives: none -> 13.9 us  [summed_here(): parts = lax.all_gather(block, axis, axis=0, tiled=False)]
    unnamed x1, blocking collectives: 72.1 us -> 68.6 us
where the time goes in v1:
time: 260 us; the launch traced here: 259 us
  blocking collectives  139 us (53%)
  matrix products  67.9 us (26%)
  other arithmetic  20.8 us (8%)
  between operations  14.1 us (5%)
  waiting for transfers between devices  13.5 us (5%)
  local copies, waits for them, and re-layouts  2.74 us (1%)
    unnamed x1, blocking collectives  68.6 us
    all_gather x2, blocking collectives, merged(): gathered = jax.tree.map(lambda a: lax.all_gather(a, axis), part)  38.2 us
    dot_general x1, matrix products, attend(): jnp.einsum('bhc,btc->bht', query, cache, preferred_element_type=jnp.float32)  28.7 us
    dot_general x1, matrix products, attend(): jnp.einsum('bht,btl->bhl', weight.astype(jnp.bfloat16), cache[:, :, :LAT]...  27.1 us
    all_gather x1, blocking collectives, body(): features = lax.all_gather(attn_out, 'ctx', axis=1, tiled=True)  18.1 us
    add x15, other arithmetic, join_partials(): summed = first[2] * left[..., None] + second[2] * right[..., None]  16.1 us
    all_gather x1, blocking collectives, summed_here(): parts = lax.all_gather(block, axis, axis=0, tiled=False)  13.9 us
    all_gather x1, waiting for transfers between devices, merged(): gathered = jax.tree.map(lambda a: lax.all_gather(a, axis), part)  13.5 us
  transfers between devices with their start and end apart: 1, of which 1 were waited for; matrix products, arithmetic and copies ran while one was open for 1% of the time, Pallas kernels for 0%

profile of v1, /device:TPU:1, one launch (start us, length us, event | category | flops | bytes accessed | tf_op | source)
XLA Modules:
  0.0 258.6 jit_solution(7811709030089921073)
XLA Ops:
  7.2 0.0 copy-start
  7.2 0.0 all-gather.7.cloned.1.call-start
  7.2 0.9 copy.20
  8.2 0.8 broadcast_compare_fusion
  8.9 0.0 copy-done
  8.9 1.1 fusion.16
  10.1 28.7 %select_reduce_fusion = (f32[8,16]{1,0:T(8,128)S(1)}, f32[8,16,8192]{2,1,0:T(8,128)}) fusion(pred[8,8192]{1,0:T(8,128)(4,1)S(1)} %broadcast_compare_fusion, bf16[8,8192,576]{1,2,0:T(8,128)(2,1)} %param.16, bf16[8,16,576]{2,0,1:T(8,128)(2,1)S(1)} %pad_maximum_fusion), kind=kOutput, calls=%fused_computation.13 | convolution fusion | flops 1211105152 | bytes 79905280 | tf_op jit(solution)/shard_map/bhc,btc->bht/dot_general | solution.py:41
  38.8 27.1 %fusion.3 = f32[8,16,512]{2,1,0:T(8,128)} fusion(bf16[8,8192,576]{1,2,0:T(8,128)(2,1)} %param.16, f32[8,16,8192]{2,1,0:T(8,128)} %get-tuple-element.200, f32[8,16]{1,0:T(8,128)S(1)} %get-tuple-element.199, pred[8,8192]{1,0:T(8,128)(4,1)S(1)} %broadcast_compare_fusion), kind=kOutput, calls=%fused_computation.8 | convolution fusion | flops 1076887552 | bytes 71631360 | tf_op jit(solution)/shard_map/bht,btl->bhl/dot_general | solution.py:46
  65.9 0.0 copy-start.2
  65.9 0.0 copy-start.3
  65.9 0.0 all-gather.7.cloned.1.call-update
  66.0 19.7 %all-gather = f32[128,16]{1,0:T(8,128)S(1)} all-gather(f32[8,16]{1,0:T(8,128)S(1)} %get-tuple-element.199), channel_id=2, replica_groups=mesh['ctx'=16,'head'=8] {'ctx'}, dimensions={0}, use_global_device_ids=true | all-gather | bytes 8704 | tf_op jit(solution)/shard_map/all_gather | solution.py:18
  85.7 3.3 %fusion.11 = f32[8,16]{1,0:T(8,128)S(1)} fusion(f32[8,16,8192]{2,1,0:T(8,128)} %get-tuple-element.200, f32[8,16]{1,0:T(8,128)S(1)} %get-tuple-element.199, pred[8,8192]{1,0:T(8,128)(4,1)S(1)} %broadcast_compare_fusion), kind=kLoop, calls=%fused_computation.20 | loop fusion | flops 3145600 | bytes 4260864 | tf_op jit(solution)/shard_map/reduce_sum | solution.py:45
  89.0 18.5 %all-gather.1 = f32[128,16]{1,0:T(8,128)S(1)} all-gather(f32[8,16]{1,0:T(8,128)S(1)} %fusion.11), channel_id=3, replica_groups=mesh['ctx'=16,'head'=8] {'ctx'}, dimensions={0}, use_global_device_ids=true | all-gather | bytes 8704 | tf_op jit(solution)/shard_map/all_gather | solution.py:18
  107.5 0.0 copy-done.2
  107.5 0.0 copy-done.3
  107.5 0.1 select_reduce_fusion.1
  107.6 13.5 %all-gather.7.cloned.1.call-done = f32[128,16,512]{2,1,0:T(8,128)} async-done(((f32[8,16,512]{2,1,0:T(8,128)}), f32[128,16,512]{2,1,0:T(8,128)}) %all-gather.7.cloned.1.call-update) | async-done | bytes 4194320 | tf_op jit(solution)/shard_map/all_gather | solution.py:18
  121.2 1.0 slice.12
  122.1 16.8 %while.19 = (s32[]{:T(128)}, f32[8,16]{1,0:T(8,128)S(1)}, f32[8,16]{1,0:T(8,128)S(1)}, f32[8,16,512]{2,1,0:T(8,128)S(1)}, f32[16,8,16]{2,1,0:T(8,128)S(1)}, /*in...) while((s32[]{:T(128)}, f32[8,16]{1,0:T(8,128)S(1)}, ...), condition=%wide.region_3.4_spmd, body=%wide.region_2.3_spmd.sunk | while | flops 197381 | bytes 791703 | solution.py:23
  122.2 1.1 fusion.47
  123.3 1.1 fusion.47
  124.4 1.1 fusion.47
  125.5 1.1 fusion.47
  126.7 1.1 fusion.47
  127.8 1.1 fusion.47
  128.9 1.1 fusion.47
  130.0 1.1 fusion.47
  131.1 1.1 fusion.47
  132.3 1.1 fusion.47
  133.4 1.1 fusion.47
  134.5 1.1 fusion.47
  135.6 1.1 fusion.47
  136.7 1.1 fusion.47
  137.9 1.1 fusion.47
  139.0 0.1 divide_convert_fusion
  139.1 3.0 %fusion.26 = f32[8,448]{1,0:T(8,128)S(1)} fusion(bf16[2048,448]{0,1:T(8,128)(2,1)} %param.20, bf16[16,512,128]{2,1,0:T(8,128)(2,1)} %param.19, bf16[8,16,512]{2,1,0:T(8,128)(2,1)S(1)} %divide_convert_fusion), kind=kOutput, calls=%fused_computation.30 | convolution fusion | flops 31473664 | bytes 4077568 | tf_op jit(solution)/shard_map/dot_general | solution.py:86
  142.1 13.9 %all-gather.3 = f32[64,448]{1,0:T(8,128)S(1)} all-gather(f32[8,448]{1,0:T(8,128)S(1)} %fusion.26), channel_id=5, replica_groups=mesh['ctx'=16,'head'=8] {'head'}, dimensions={0}, use_global_device_ids=true | all-gather | bytes 129024 | tf_op jit(solution)/shard_map/all_gather | solution.py:12
  156.0 0.0 copy-start.1
  156.0 18.1 %all-gather.4 = bf16[16,448,8]{1,2,0:T(8,128)(2,1)S(1)} all-gather(bf16[1,448,8]{1,2,0:T(8,128)(2,1)S(1)} %bitcast.61), channel_id=1, replica_groups=mesh['ctx'=16,'head'=8] {'ctx'}, dimensions={0}, use_global_device_ids=true | all-gather | bytes 121856 | tf_op jit(solution)/shard_map/all_gather | solution.py:88
  174.2 0.1 reshape.66
  174.4 0.2 multiply_reduce_fusion
  174.6 2.7 %fusion.8 = f32[8,256]{1,0:T(8,128)S(1)} fusion(bf16[1,7168,256]{2,1,0:T(8,128)(2,1)} %param.21, f32[7168,8]{0,1:T(8,128)S(1)} %reshape.66, f32[8]{0:T(128)S(1)} %add_sqrt_fusion), kind=kOutput, calls=%fused_computation.17 | convolution fusion | flops 29474816 | bytes 3907616 | tf_op jit(solution)/shard_map/dot_general | solution.py:95
  177.2 5.3 %convolution_multiply_fusion.1 = f32[8,7168]{1,0:T(8,128)S(1)} fusion(bf16[1,256,7168]{2,1,0:T(8,128)(2,1)} %param.23, bf16[1,7168,256]{2,1,0:T(8,128)(2,1)} %param.22, f32[8]{0:T(128)S(1)} %select_reduce_fusion.1, f32[8,256]{1,0:T(8,128)S(1)} %fusion.8, f32[7168,8]{0,1:T(8,128)S(1)} %reshape.66, f32[8]{0:T(128)S(1)} %add_sqrt_fusion), kind=kOutput, calls=%fused_computation.11 | convolution fusion | flops 58904576 | bytes 7807040 | tf_op jit(solution)/shard_map/dot_general | solution.py:98
  182.5 0.0 copy-done.1
  182.5 68.6 %all-reduce.2 = bf16[8,7168]{1,0:T(8,128)(2,1)S(1)} all-reduce(f32[8,7168]{1,0:T(8,128)S(1)} %convolution_multiply_fusion.1), channel_id=6, replica_groups=mesh['ctx'=16,'head'=8] {'ctx','head'}, use_global_device_ids=true, to_apply=%region_7.8.clone | all-reduce | flops 57344 | bytes 344064
  251.1 0.7 dynamic-slice_convert_fusion
  (22 shorter events, 0.4 us)
Async XLA Ops:
  7.2 1.8 copy-start
  7.2 114.0 %all-gather.7.cloned.1.call-start = ((), (), s32[]{:S(2)}) async-start(), calls=%async_computation | async-start | bytes 4456448 | tf_op jit(solution)/shard_map/all_gather | solution.py:18
  65.9 41.6 %copy-start.2 = (f32[8,8]{1,0:T(8,128)S(1)}, f32[8,8]{1,0:T(8,128)}, u32[]{:S(2)}) copy-start(f32[8,8]{1,0:T(8,128)} %param.25) | copy-start | bytes 772
  65.9 41.6 %copy-start.3 = (s32[8,8]{1,0:T(8,128)S(1)}, s32[8,8]{1,0:T(8,128)}, u32[]{:S(2)}) copy-start(s32[8,8]{1,0:T(8,128)} %param.24) | copy-start | bytes 772
  156.0 26.5 %copy-start.1 = (bf16[8,448]{1,0:T(8,128)(2,1)}, bf16[8,448]{1,0:T(8,128)(2,1)S(1)}, u32[]{:S(2)}) copy-start(bf16[8,448]{1,0:T(8,128)(2,1)S(1)} %bitcast_reduce_fusion) | copy-start | bytes 21508
Sparse Core Ops, SparseCore 0:
  66.1 55.0 all-gather.6
